TPU v7x, 32 devices: a whole 2x2x4 slice. The times are simulated.
32 devices in a mesh: node: 8 (over y, x, core), dev: 4 (over z).
Axes of the slice: x: 2, y: 2, z: 4, core: 2. Of those that a mesh axis runs over, the one named last changes fastest.
Arguments:
- tokens: bfloat16 [128, 4096], P('node', 'dev'), may hold values from -6 to 6
- routes: int32 [128, 8], P('node'), may hold values from 0 to 7, as said below
- gate_codes: int32 [128, 8], P('node'), may hold values from 1 to 65535
- w_gate: bfloat16 [8, 4096, 2048], P('node', None, 'dev'), may hold values from -0.09375 to 0.09375
- w_up: bfloat16 [8, 4096, 2048], P('node', None, 'dev'), may hold values from -0.09375 to 0.09375
- w_down: bfloat16 [8, 2048, 4096], P('node', 'dev'), may hold values from -0.125 to 0.125
- cotangent: bfloat16 [128, 4096], P('node', 'dev'), may hold values from -6 to 6
Outputs:
- layer_out: bfloat16 [128, 4096], P('node', 'dev')
- token_grad: bfloat16 [128, 4096], P('node', 'dev')
- down_grad: bfloat16 [8, 2048, 4096], P('node', 'dev')
Inputs may be any that keep to these rules, and one draw needn't show every extreme that they name: `routes`: each token names 8 different experts, taken from at most 4 groups of 4 consecutive experts. Among the 16 tokens of one block (one index of node), no expert is named by more than 16 tokens, and in every block some expert is named by exactly 16.
All inputs are finite; a program needn't handle non-finite values.
Results may differ from a plain program's by a relative error of at most 0.012.
Values may be sent and summed in bfloat16 or wider, within the bound.
A program may use at most 64 MiB of HBM per device.

v0:
```python
import jax
import jax.numpy as jnp
from jax import lax
from jax.sharding import PartitionSpec as P

TOP_GROUPS = 4
GROUP_SIZE = 4
exact_mode = lax.Precision.HIGHEST


def slot_layout(routes, gate_codes, experts, capacity):
    tokens_here = routes.shape[0]
    member = (routes[:, :, None] == jnp.arange(experts, dtype=jnp.int32)[None, None, :]).astype(
        jnp.float32
    )
    named_by = jnp.sum(member, axis=1)
    earlier = (jnp.arange(tokens_here)[:, None] > jnp.arange(tokens_here)[None, :]).astype(
        jnp.float32
    )
    before = jnp.dot(earlier, named_by, precision=exact_mode)
    placed = named_by[:, :, None] * (
        before[:, :, None] == jnp.arange(capacity).astype(jnp.float32)[None, None, :]
    ).astype(jnp.float32)
    weights = gate_codes.astype(jnp.float32) / 65536.0
    gating = jnp.sum(member * weights[:, :, None], axis=1)
    return (placed, gating)


def deliver(local_rows, build, fold, initial):
    whole_rows = lax.all_gather(local_rows, "dev", axis=1, tiled=True)
    arrived = lax.all_to_all(build(whole_rows), "node", split_axis=0, concat_axis=0, tiled=True)
    return fold(initial, arrived, 0)


def send_back(partial_value):
    shares = lax.psum_scatter(
        partial_value.astype(jnp.bfloat16), "dev", scatter_dimension=2, tiled=True
    )
    return lax.all_to_all(shares, "node", split_axis=0, concat_axis=0, tiled=True)


def on_device(tokens, routes, gate_codes, w_gate, w_up, w_down, cotangent):
    experts = lax.axis_size("node")
    groups = experts // GROUP_SIZE
    chosen_count = min(TOP_GROUPS, groups)
    capacity = tokens.shape[0] * chosen_count // groups
    placed, gating = slot_layout(routes, gate_codes, experts, capacity)
    place_low = placed.astype(jnp.bfloat16)
    weighted = placed * gating[:, :, None]
    gate_mat = w_gate[0]
    up_mat = w_up[0]
    down_mat = w_down[0]
    hidden_width = gate_mat.shape[1]

    def spread_tokens(payload):
        return jnp.einsum(
            "tep,tf->epf", place_low, payload, preferred_element_type=jnp.float32
        ).astype(jnp.bfloat16)

    def spread_cotangent(payload):
        return jnp.einsum(
            "tep,tf->epf", weighted, payload.astype(jnp.float32), precision=exact_mode
        ).astype(jnp.bfloat16)

    def project_in(totals, portion, offset):
        gate_next = jnp.einsum("epf,fh->eph", portion, gate_mat, preferred_element_type=jnp.float32)
        up_next = jnp.einsum("epf,fh->eph", portion, up_mat, preferred_element_type=jnp.float32)
        return (gate_next, up_next)

    empty_hidden = jnp.zeros((experts, capacity, hidden_width), jnp.float32)
    gate_pre, up_pre = deliver(tokens, spread_tokens, project_in, (empty_hidden, empty_hidden))
    squash = jax.nn.sigmoid(gate_pre)
    hidden = (gate_pre * squash * up_pre).astype(jnp.bfloat16)
    partial_value = jnp.einsum("eph,hf->epf", hidden, down_mat, preferred_element_type=jnp.float32)
    returned = send_back(partial_value)
    layer_out = jnp.einsum(
        "tep,epf->tf", weighted, returned.astype(jnp.float32), precision=exact_mode
    ).astype(jnp.bfloat16)

    def project_cotangent(totals, portion, offset):
        grad_next = jnp.einsum("epf,hf->eph", portion, down_mat, preferred_element_type=jnp.float32)
        block_grad = jnp.einsum("eph,epf->hf", hidden, portion, preferred_element_type=jnp.float32)
        return (grad_next, block_grad)

    empty_down = jnp.zeros((hidden_width, down_mat.shape[1]), jnp.float32)
    hidden_grad, down_total = deliver(
        cotangent, spread_cotangent, project_cotangent, (empty_hidden, empty_down)
    )
    gate_grad = (hidden_grad * up_pre * squash * (1.0 + gate_pre * (1.0 - squash))).astype(
        jnp.bfloat16
    )
    up_grad = (hidden_grad * gate_pre * squash).astype(jnp.bfloat16)
    partial_back = jnp.einsum(
        "eph,fh->epf", gate_grad, gate_mat, preferred_element_type=jnp.float32
    )
    partial_back = partial_back + jnp.einsum(
        "eph,fh->epf", up_grad, up_mat, preferred_element_type=jnp.float32
    )
    returned_back = send_back(partial_back)
    token_grad = jnp.einsum(
        "tep,epf->tf", placed, returned_back.astype(jnp.float32), precision=exact_mode
    ).astype(jnp.bfloat16)
    return (layer_out, token_grad, down_total.astype(jnp.bfloat16)[None])


def solution(mesh):
    in_specs = (
        P("node", "dev"),
        P("node", None),
        P("node", None),
        P("node", None, "dev"),
        P("node", None, "dev"),
        P("node", "dev", None),
        P("node", "dev"),
    )
    out_specs = (P("node", "dev"), P("node", "dev"), P("node", "dev", None))
    return jax.shard_map(
        on_device, mesh=mesh, in_specs=in_specs, out_specs=out_specs, check_vma=False
    )
```

profile of v0, /device:TPU:0, one launch (start us, length us, event | category | flops | bytes accessed | tf_op | source)
XLA Modules:
  0.0 132.5 jit_solution(16287439819941731388)
XLA Ops:
  7.2 0.7 convert_multiply_fusion
  7.9 0.7 select_reduce_fusion
  8.6 0.1 fusion.38
  8.7 15.3 %all_gather.6 = bf16[16,4096]{1,0:T(8,128)(2,1)S(1)} all-gather(bf16[16,1024]{1,0:T(8,128)(2,1)} %param.7), channel_id=1, replica_groups=mesh['node'=8,'dev'=4] {'dev'}, dimensions={1}, use_global_device_ids=true | all-gather | bytes 163840 | tf_op jit(solution)/shard_map/all_gather | solution.py:30
  24.0 1.5 %convolution_convert_fusion.2 = bf16[8,16,4096]{2,1,0:T(8,128)(2,1)} fusion(bf16[16,4096]{1,0:T(8,128)(2,1)S(1)} %all_gather.6, f32[16,8]{0,1:T(8,128)S(1)} %get-tuple-element.4, f32[16]{0:T(128)S(1)} %iota_convert_fusion, f32[16,8]{0,1:T(8,128)S(1)} %fusion.38), kind=kOutput, calls=%fused_computation.6 | convolution fusion | flops 17305600 | bytes 1180736 | tf_op jit(solution)/shard_map/tep,tf->epf/dot_general | solution.py:56
  25.5 3.7 %all-to-all-start = ((bf16[8,16,4096]{2,1,0:T(8,128)(2,1)}), bf16[8,16,4096]{2,1,0:T(8,128)(2,1)S(1)}, u32[]{:S(2)}, u32[]{:S(2)}) async-start(bf16[8,16,4096]{2,1,0:T(8,128)(2,1)} %convolution_convert_fusion.2), calls=%async_computation | async-start | bytes 2097152 | tf_op jit(solution)/shard_map/all_to_all | solution.py:31
  29.2 13.7 %all_gather.7 = bf16[16,4096]{1,0:T(8,128)(2,1)S(1)} all-gather(bf16[16,1024]{1,0:T(8,128)(2,1)} %param.13), channel_id=1, replica_groups=mesh['node'=8,'dev'=4] {'dev'}, dimensions={1}, use_global_device_ids=true | all-gather | bytes 163840 | tf_op jit(solution)/shard_map/all_gather | solution.py:30
  42.8 2.1 %convolution_convert_fusion = bf16[8,16,4096]{2,1,0:T(8,128)(2,1)} fusion(bf16[16,4096]{1,0:T(8,128)(2,1)S(1)} %all_gather.7, f32[16,8]{0,1:T(8,128)S(1)} %get-tuple-element.3, f32[16,8]{0,1:T(8,128)S(1)} %get-tuple-element.4, f32[16]{0:T(128)S(1)} %iota_convert_fusion, f32[16,8]{0,1:T(8,128)S(1)} %fusion.38), kind=kOutput, calls=%fused_computation.4 | convolution fusion | flops 101193728 | bytes 1181248 | tf_op jit(solution)/shard_map/tep,tf->epf/dot_general | solution.py:61
  44.9 0.0 all-to-all-done
  44.9 4.1 %all-to-all-start.2 = ((bf16[8,16,4096]{2,1,0:T(8,128)(2,1)}), bf16[8,16,4096]{2,1,0:T(8,128)(2,1)S(1)}, u32[]{:S(2)}, u32[]{:S(2)}) async-start(bf16[8,16,4096]{2,1,0:T(8,128)(2,1)} %convolution_convert_fusion), calls=%async_computation.3 | async-start | bytes 2097152 | tf_op jit(solution)/shard_map/all_to_all | solution.py:31
  49.0 0.0 reduce-scatter.3.cloned.1.call-start
  49.1 0.0 copy-start.2
  49.1 3.1 %fusion.10 = f32[8,16,512]{2,1,0:T(8,128)S(1)} fusion(bf16[8,16,4096]{2,1,0:T(8,128)(2,1)S(1)} %all-to-all-done, bf16[1,4096,512]{2,1,0:T(8,128)(2,1)} %param.10), kind=kOutput, calls=%fused_computation.15 | convolution fusion | flops 536870912 | bytes 5505024 | tf_op jit(solution)/shard_map/epf,fh->eph/dot_general | solution.py:66
  52.1 0.4 copy-done.2
  52.5 0.0 copy-start
  52.5 0.8 multiply_convert_fusion.2
  53.3 1.4 %copy-done = bf16[1,512,4096]{2,1,0:T(8,128)(2,1)S(1)} copy-done((bf16[1,512,4096]{2,1,0:T(8,128)(2,1)S(1)}, bf16[1,512,4096]{2,1,0:T(8,128)(2,1)}, u32[]{:S(2)}) %copy-start) | copy-done | bytes 4194328
  54.7 1.7 %convolution_convert_fusion.1 = bf16[8,16,4096]{2,1,0:T(8,128)(2,1)} fusion(bf16[8,16,512]{2,1,0:T(8,128)(2,1)S(1)} %get-tuple-element.5, bf16[1,512,4096]{2,1,0:T(8,128)(2,1)S(1)} %copy-done), kind=kOutput, calls=%fused_computation.5 | convolution fusion | flops 537395200 | bytes 5373952 | tf_op jit(solution)/shard_map/eph,hf->epf/dot_general | solution.py:74
  56.4 0.0 reduce-scatter.3.cloned.1.call-update
  56.5 0.0 reduce-scatter.5.cloned.1.call-start
  56.5 7.9 %all-to-all-done.2 = bf16[8,16,4096]{2,1,0:T(8,128)(2,1)S(1)} async-done(((bf16[8,16,4096]{2,1,0:T(8,128)(2,1)}), bf16[8,16,4096]{2,1,0:T(8,128)(2,1)S(1)}, u32[]{:S(2)}, u32[]{:S(2)}) %all-to-all-start.2) | async-done | bytes 1048608 | tf_op jit(solution)/shard_map/all_to_all | solution.py:31
  64.4 0.0 copy-start.1
  64.4 3.9 %fusion.2 = f32[8,16,512]{2,1,0:T(8,128)S(1)} fusion(bf16[8,16,4096]{2,1,0:T(8,128)(2,1)S(1)} %all-to-all-done.2, bf16[1,512,4096]{2,1,0:T(8,128)(2,1)} %param.12), kind=kOutput, calls=%fused_computation.7 | convolution fusion | flops 536870912 | bytes 5505024 | tf_op jit(solution)/shard_map/epf,hf->eph/dot_general | solution.py:81
  68.3 0.0 copy-start.3
  68.3 0.0 copy-done.1
  68.3 1.5 %fusion.8 = f32[8,16,4096]{2,1,0:T(8,128)S(1)} fusion(bf16[1,4096,512]{2,1,0:T(8,128)(2,1)S(1)} %copy-done.1, f32[8,16,512]{2,1,0:T(8,128)S(1)} %fusion.10, f32[8,16,512]{2,1,0:T(8,128)S(1)} %fusion.2, f32[8,16,512]{2,1,0:T(8,128)S(1)} %get-tuple-element.6), kind=kOutput, calls=%fused_computation.13 | convolution fusion | flops 537526272 | bytes 7077888 | tf_op jit(solution)/shard_map/eph,fh->epf/dot_general | solution.py:93
  69.8 0.7 copy-done.3
  70.5 2.5 %fusion.1 = bf16[8,16,4096]{2,1,0:T(8,128)(2,1)} fusion(f32[8,16,4096]{2,1,0:T(8,128)S(1)} %fusion.8, bf16[1,4096,512]{2,1,0:T(8,128)(2,1)S(1)} %copy-done.3, f32[8,16,512]{2,1,0:T(8,128)S(1)} %fusion.2, f32[8,16,512]{2,1,0:T(8,128)S(1)} %fusion.10), kind=kOutput, calls=%fused_computation.3 | convolution fusion | flops 538312704 | bytes 7864320 | tf_op jit(solution)/shard_map/eph,fh->epf/dot_general | solution.py:96
  73.0 0.0 reduce-scatter.5.cloned.1.call-update
  73.0 12.7 %reduce-scatter.3.cloned.1.call-done = bf16[8,16,1024]{2,1,0:T(8,128)(2,1)} async-done(((bf16[8,16,4096]{2,1,0:T(8,128)(2,1)}), bf16[8,16,1024]{2,1,0:T(8,128)(2,1)}) %reduce-scatter.3.cloned.1.call-update) | async-done | bytes 262160 | tf_op jit(solution)/shard_map/reduce_scatter | solution.py:36
  85.7 3.6 %all-to-all-start.1 = ((bf16[8,16,1024]{2,1,0:T(8,128)(2,1)}), bf16[8,16,1024]{2,1,0:T(8,128)(2,1)S(1)}, u32[]{:S(2)}, u32[]{:S(2)}) async-start(bf16[8,16,1024]{2,1,0:T(8,128)(2,1)} %reduce-scatter.3.cloned.1.call-done), calls=%async_computation.2 | async-start | bytes 524288 | tf_op jit(solution)/shard_map/all_to_all | solution.py:39
  89.3 3.3 %fusion = bf16[1,512,4096]{2,1,0:T(8,128)(2,1)} fusion(bf16[8,16,512]{2,1,0:T(8,128)(2,1)S(1)} %get-tuple-element.5, bf16[8,16,4096]{2,1,0:T(8,128)(2,1)S(1)} %all-to-all-done.2), kind=kOutput, calls=%fused_computation.1 | convolution fusion | flops 538968064 | bytes 5373952 | tf_op jit(solution)/shard_map/eph,epf->hf/dot_general | solution.py:82
  92.6 21.3 %reduce-scatter.5.cloned.1.call-done = bf16[8,16,1024]{2,1,0:T(8,128)(2,1)} async-done(((bf16[8,16,4096]{2,1,0:T(8,128)(2,1)}), bf16[8,16,1024]{2,1,0:T(8,128)(2,1)}) %reduce-scatter.5.cloned.1.call-update) | async-done | bytes 262160 | tf_op jit(solution)/shard_map/reduce_scatter | solution.py:36
  113.9 0.0 all-to-all-done.1
  113.9 3.6 %all-to-all-start.3 = ((bf16[8,16,1024]{2,1,0:T(8,128)(2,1)}), bf16[8,16,1024]{2,1,0:T(8,128)(2,1)S(1)}, u32[]{:S(2)}, u32[]{:S(2)}) async-start(bf16[8,16,1024]{2,1,0:T(8,128)(2,1)} %reduce-scatter.5.cloned.1.call-done), calls=%async_computation.5 | async-start | bytes 524288 | tf_op jit(solution)/shard_map/all_to_all | solution.py:39
  117.6 1.1 fusion.12
  118.7 5.8 %all-to-all-done.3 = bf16[8,16,1024]{2,1,0:T(8,128)(2,1)S(1)} async-done(((bf16[8,16,1024]{2,1,0:T(8,128)(2,1)}), bf16[8,16,1024]{2,1,0:T(8,128)(2,1)S(1)}, u32[]{:S(2)}, u32[]{:S(2)}) %all-to-all-start.3) | async-done | bytes 262176 | tf_op jit(solution)/shard_map/all_to_all | solution.py:39
  124.5 1.1 fusion.13
  (1 shorter events, 0.0 us)
Async XLA Ops:
  25.5 19.5 %all-to-all-start = ((bf16[8,16,4096]{2,1,0:T(8,128)(2,1)}), bf16[8,16,4096]{2,1,0:T(8,128)(2,1)S(1)}, u32[]{:S(2)}, u32[]{:S(2)}) async-start(bf16[8,16,4096]{2,1,0:T(8,128)(2,1)} %convolution_convert_fusion.2), calls=%async_computation | async-start | bytes 2097152 | tf_op jit(solution)/shard_map/all_to_all | solution.py:31
  44.9 19.5 %all-to-all-start.2 = ((bf16[8,16,4096]{2,1,0:T(8,128)(2,1)}), bf16[8,16,4096]{2,1,0:T(8,128)(2,1)S(1)}, u32[]{:S(2)}, u32[]{:S(2)}) async-start(bf16[8,16,4096]{2,1,0:T(8,128)(2,1)} %convolution_convert_fusion), calls=%async_computation.3 | async-start | bytes 2097152 | tf_op jit(solution)/shard_map/all_to_all | solution.py:31
  49.0 36.7 %reduce-scatter.3.cloned.1.call-start = ((), (), s32[]{:S(2)}) async-start(), calls=%async_computation.6 | async-start | bytes 1310720 | tf_op jit(solution)/shard_map/reduce_scatter | solution.py:36
  49.1 3.5 %copy-start.2 = (bf16[1,4096,512]{2,1,0:T(8,128)(2,1)S(1)}, bf16[1,4096,512]{2,1,0:T(8,128)(2,1)}, u32[]{:S(2)}) copy-start(bf16[1,4096,512]{2,1,0:T(8,128)(2,1)} %param.11) | copy-start | bytes 12582916
  52.5 2.2 %copy-start = (bf16[1,512,4096]{2,1,0:T(8,128)(2,1)S(1)}, bf16[1,512,4096]{2,1,0:T(8,128)(2,1)}, u32[]{:S(2)}) copy-start(bf16[1,512,4096]{2,1,0:T(8,128)(2,1)} %param.12) | copy-start | bytes 12582916
  56.5 57.5 %reduce-scatter.5.cloned.1.call-start = ((), (), s32[]{:S(2)}) async-start(), calls=%async_computation.7 | async-start | bytes 1310720 | tf_op jit(solution)/shard_map/reduce_scatter | solution.py:36
  64.4 3.9 %copy-start.1 = (bf16[1,4096,512]{2,1,0:T(8,128)(2,1)S(1)}, bf16[1,4096,512]{2,1,0:T(8,128)(2,1)}, u32[]{:S(2)}) copy-start(bf16[1,4096,512]{2,1,0:T(8,128)(2,1)} %param.10) | copy-start | bytes 12582916
  68.3 2.2 %copy-start.3 = (bf16[1,4096,512]{2,1,0:T(8,128)(2,1)S(1)}, bf16[1,4096,512]{2,1,0:T(8,128)(2,1)}, u32[]{:S(2)}) copy-start(bf16[1,4096,512]{2,1,0:T(8,128)(2,1)} %param.11) | copy-start | bytes 12582916
  85.7 28.2 %all-to-all-start.1 = ((bf16[8,16,1024]{2,1,0:T(8,128)(2,1)}), bf16[8,16,1024]{2,1,0:T(8,128)(2,1)S(1)}, u32[]{:S(2)}, u32[]{:S(2)}) async-start(bf16[8,16,1024]{2,1,0:T(8,128)(2,1)} %reduce-scatter.3.cloned.1.call-done), calls=%async_computation.2 | async-start | bytes 524288 | tf_op jit(solution)/shard_map/all_to_all | solution.py:39
  113.9 10.6 %all-to-all-start.3 = ((bf16[8,16,1024]{2,1,0:T(8,128)(2,1)}), bf16[8,16,1024]{2,1,0:T(8,128)(2,1)S(1)}, u32[]{:S(2)}, u32[]{:S(2)}) async-start(bf16[8,16,1024]{2,1,0:T(8,128)(2,1)} %reduce-scatter.5.cloned.1.call-done), calls=%async_computation.5 | async-start | bytes 524288 | tf_op jit(solution)/shard_map/all_to_all | solution.py:39
Sparse Core Ops, SparseCore 0:
  56.6 29.0 reduce-scatter.2
  88.1 25.7 reduce-scatter.4
where the time goes:
time: 133 us; the launch traced here: 132 us
  waiting for transfers between devices  47.7 us (36%)
  blocking collectives  28.9 us (22%)
  matrix products  22.7 us (17%)
  starting transfers between devices  15.2 us (11%)
  between operations  14.1 us (11%)
  local copies, waits for them, and re-layouts  2.48 us (2%)
  other arithmetic  1.4 us (1%)
    reduce_scatter x2, waiting for transfers between devices, send_back(): lax.psum_scatter(partial_value.astype(jnp.bfloat16), 'dev', scatter_dimen...  34 us
    all_gather x2, blocking collectives, deliver(): whole_rows = lax.all_gather(local_rows, 'dev', axis=1, tiled=True)  28.9 us
    all_to_all x2, waiting for transfers between devices, deliver(): lax.all_to_all(build(whole_rows), 'node', split_axis=0, concat_axis=0, ti...  7.91 us
    all_to_all x2, starting transfers between devices, deliver(): lax.all_to_all(build(whole_rows), 'node', split_axis=0, concat_axis=0, ti...  7.81 us
    all_to_all x2, starting transfers between devices, send_back(): lax.all_to_all(shares, 'node', split_axis=0, concat_axis=0, tiled=True)  7.29 us
    all_to_all x2, waiting for transfers between devices, send_back(): lax.all_to_all(shares, 'node', split_axis=0, concat_axis=0, tiled=True)  5.79 us
    dot_general x1, matrix products, project_cotangent(): jnp.einsum('epf,hf->eph', portion, down_mat, preferred_element_type=jnp.f...  3.88 us
    dot_general x1, matrix products, project_cotangent(): jnp.einsum('eph,epf->hf', hidden, portion, preferred_element_type=jnp.flo...  3.29 us
  transfers between devices with their start and end apart: 6, of which 4 were waited for; matrix products, arithmetic and copies ran while one was open for 15% of the time, Pallas kernels for 0%

commit v1 on v0

--- a/solution.py
+++ b/solution.py
@@ -27,7 +27,13 @@
 
 
 def deliver(local_rows, build, fold, initial):
-    whole_rows = lax.all_gather(local_rows, "dev", axis=1, tiled=True)
+    size = lax.axis_size("dev")
+    current, tiles = (local_rows, [local_rows])
+    for _ in range(size - 1):
+        current = lax.ppermute(current, "dev", [(i, (i + 1) % size) for i in range(size)])
+        tiles.insert(0, current)
+    line = jnp.concatenate(tiles, axis=1)
+    whole_rows = jnp.roll(line, (lax.axis_index("dev") + 1) * local_rows.shape[1], axis=1)
     arrived = lax.all_to_all(build(whole_rows), "node", split_axis=0, concat_axis=0, tiled=True)
     return fold(initial, arrived, 0)
 

time: 133 us -> 138 us (1.038)
  blocking collectives: 28.9 us -> 0 us
  waiting for transfers between devices: 47.7 us -> 75.8 us
  starting transfers between devices: 15.2 us -> 18.6 us
  matrix products: 22.7 us -> 24.8 us
    ppermute x0 -> x6, waiting for transfers between devices: none -> 31.4 us  [deliver(): lax.ppermute(current, 'dev', [(i, (i + 1) % size) for i in range(size)])]
    all_gather x2 -> x0, blocking collectives: 28.9 us -> none  [deliver(): whole_rows = lax.all_gather(local_rows, 'dev', axis=1, tiled=True)]
    reduce_scatter x2, waiting for transfers between devices: 34 us -> 30.6 us  [send_back(): lax.psum_scatter(partial_value.astype(jnp.bfloat16), 'dev', scatter_dimen...]
    ppermute x0 -> x6, starting transfers between devices: none -> 3.09 us  [deliver(): lax.ppermute(current, 'dev', [(i, (i + 1) % size) for i in range(size)])]
  transfers between devices with their start and end apart: 6 -> 12, of which waited for: 4 -> 10; matrix products, arithmetic and copies ran while one was open for 15% -> 16% of each run, Pallas kernels for 0% -> 0%
where the time goes in v1:
time: 138 us; the launch traced here: 137 us
  waiting for transfers between devices  75.8 us (55%)
  matrix products  24.8 us (18%)
  starting transfers between devices  18.6 us (13%)
  between operations  14.1 us (10%)
  local copies, waits for them, and re-layouts  2.49 us (2%)
  other arithmetic  1.39 us (1%)
    ppermute x6, waiting for transfers between devices, deliver(): lax.ppermute(current, 'dev', [(i, (i + 1) % size) for i in range(size)])  31.4 us
    reduce_scatter x2, waiting for transfers between devices, send_back(): lax.psum_scatter(partial_value.astype(jnp.bfloat16), 'dev', scatter_dimen...  30.6 us
    all_to_all x2, starting transfers between devices, deliver(): lax.all_to_all(build(whole_rows), 'node', split_axis=0, concat_axis=0, ti...  8.13 us
    all_to_all x2, waiting for transfers between devices, deliver(): lax.all_to_all(build(whole_rows), 'node', split_axis=0, concat_axis=0, ti...  7.92 us
    all_to_all x2, starting transfers between devices, send_back(): lax.all_to_all(shares, 'node', split_axis=0, concat_axis=0, tiled=True)  7.32 us
    all_to_all x2, waiting for transfers between devices, send_back(): lax.all_to_all(shares, 'node', split_axis=0, concat_axis=0, tiled=True)  5.79 us
    dot_general x1, matrix products, project_cotangent(): jnp.einsum('epf,hf->eph', portion, down_mat, preferred_element_type=jnp.f...  3.86 us
    dot_general x1, matrix products, project_cotangent(): jnp.einsum('eph,epf->hf', hidden, portion, preferred_element_type=jnp.flo...  3.29 us
  transfers between devices with their start and end apart: 12, of which 10 were waited for; matrix products, arithmetic and copies ran while one was open for 16% of the time, Pallas kernels for 0%

profile of v1, /device:TPU:0, one launch (start us, length us, event | category | flops | bytes accessed | tf_op | source)
XLA Modules:
  0.0 137.2 jit_solution(14461652059188065462)
XLA Ops:
  7.2 3.1 %collective-permute-start = (bf16[16,1024]{1,0:T(8,128)(2,1)}, bf16[16,1024]{1,0:T(8,128)(2,1)S(1)}, u32[]{:S(2)}, u32[]{:S(2)}) collective-permute-start(bf16[16,1024]{1,0:T(8,128)(2,1)} %param.9), channel_id=1, source_target_pairs={{0,1},{1,2},{2,3},{3,0},{4,5},{5,6},{6,7},{7,4},{8,9},{9,10},{10,1... | collective-permute-start | bytes 98312 | tf_op jit(solution)/shard_map/ppermute | solution.py:33
  10.2 0.7 convert_multiply_fusion
  10.9 0.7 select_reduce_fusion
  11.6 2.7 %collective-permute-done = bf16[16,1024]{1,0:T(8,128)(2,1)S(1)} collective-permute-done((bf16[16,1024]{1,0:T(8,128)(2,1)}, bf16[16,1024]{1,0:T(8,128)(2,1)S(1)}, u32[]{:S(2)}, u32[]{:S(2)}) %collective-permute-start) | collective-permute-done | bytes 32800 | tf_op jit(solution)/shard_map/ppermute | solution.py:33
  14.4 0.0 collective-permute-start.1
  14.4 0.1 fusion.56
  14.5 5.6 %collective-permute-done.1 = bf16[16,1024]{1,0:T(8,128)(2,1)S(1)} collective-permute-done((bf16[16,1024]{1,0:T(8,128)(2,1)S(1)}, bf16[16,1024]{1,0:T(8,128)(2,1)S(1)}, u32[]{:S(2)}, u32[]{:S(2)}) %collective-permute-start.1) | collective-permute-done | bytes 32800 | tf_op jit(solution)/shard_map/ppermute | solution.py:33
  20.1 0.0 collective-permute-start.2
  20.1 5.7 %collective-permute-done.2 = bf16[16,1024]{1,0:T(8,128)(2,1)S(1)} collective-permute-done((bf16[16,1024]{1,0:T(8,128)(2,1)S(1)}, bf16[16,1024]{1,0:T(8,128)(2,1)S(1)}, u32[]{:S(2)}, u32[]{:S(2)}) %collective-permute-start.2) | collective-permute-done | bytes 32800 | tf_op jit(solution)/shard_map/ppermute | solution.py:33
  25.8 2.6 %convolution_convert_fusion.2 = bf16[8,16,4096]{2,1,0:T(8,128)(2,1)} fusion(s32[]{:T(128)S(6)} %select_n.13, bf16[16,1024]{1,0:T(8,128)(2,1)S(1)} %collective-permute-done.2, bf16[16,1024]{1,0:T(8,128)(2,1)S(1)} %collective-permute-done.1, bf16[16,1024]{1,0:T(8,128)(2,1)S(1)} %collective-permute-done, bf16[16,1024]{1,0:T(8,128)(2,1)} %param.9, ...), kind=kOutput, calls=%fused_computation.6 | convolution fusion | flops 18354176 | bytes 1180740 | tf_op jit(solution)/shard_map/tep,tf->epf/dot_general | solution.py:62
  28.4 3.9 %all-to-all-start = ((bf16[8,16,4096]{2,1,0:T(8,128)(2,1)}), bf16[8,16,4096]{2,1,0:T(8,128)(2,1)S(1)}, u32[]{:S(2)}, u32[]{:S(2)}) async-start(bf16[8,16,4096]{2,1,0:T(8,128)(2,1)} %convolution_convert_fusion.2), calls=%async_computation | async-start | bytes 2097152 | tf_op jit(solution)/shard_map/all_to_all | solution.py:37
  32.3 0.0 collective-permute-start.3
  32.3 5.9 %collective-permute-done.3 = bf16[16,1024]{1,0:T(8,128)(2,1)S(1)} collective-permute-done((bf16[16,1024]{1,0:T(8,128)(2,1)}, bf16[16,1024]{1,0:T(8,128)(2,1)S(1)}, u32[]{:S(2)}, u32[]{:S(2)}) %collective-permute-start.3) | collective-permute-done | bytes 32800 | tf_op jit(solution)/shard_map/ppermute | solution.py:33
  38.2 0.0 collective-permute-start.4
  38.2 5.7 %collective-permute-done.4 = bf16[16,1024]{1,0:T(8,128)(2,1)S(1)} collective-permute-done((bf16[16,1024]{1,0:T(8,128)(2,1)S(1)}, bf16[16,1024]{1,0:T(8,128)(2,1)S(1)}, u32[]{:S(2)}, u32[]{:S(2)}) %collective-permute-start.4) | collective-permute-done | bytes 32800 | tf_op jit(solution)/shard_map/ppermute | solution.py:33
  43.9 0.0 collective-permute-start.5
  43.9 5.7 %collective-permute-done.5 = bf16[16,1024]{1,0:T(8,128)(2,1)S(1)} collective-permute-done((bf16[16,1024]{1,0:T(8,128)(2,1)S(1)}, bf16[16,1024]{1,0:T(8,128)(2,1)S(1)}, u32[]{:S(2)}, u32[]{:S(2)}) %collective-permute-start.5) | collective-permute-done | bytes 32800 | tf_op jit(solution)/shard_map/ppermute | solution.py:33
  49.7 3.1 %convolution_convert_fusion = bf16[8,16,4096]{2,1,0:T(8,128)(2,1)} fusion(s32[]{:T(128)S(6)} %select_n.13, bf16[16,1024]{1,0:T(8,128)(2,1)S(1)} %collective-permute-done.5, bf16[16,1024]{1,0:T(8,128)(2,1)S(1)} %collective-permute-done.4, bf16[16,1024]{1,0:T(8,128)(2,1)S(1)} %collective-permute-done.3, bf16[16,1024]{1,0:T(8,128)(2,1)} %param.15, ...), kind=kOutput, calls=%fused_computation.4 | convolution fusion | flops 102242304 | bytes 1181252 | tf_op jit(solution)/shard_map/tep,tf->epf/dot_general | solution.py:67
  52.8 0.0 all-to-all-done
  52.8 4.2 %all-to-all-start.2 = ((bf16[8,16,4096]{2,1,0:T(8,128)(2,1)}), bf16[8,16,4096]{2,1,0:T(8,128)(2,1)S(1)}, u32[]{:S(2)}, u32[]{:S(2)}) async-start(bf16[8,16,4096]{2,1,0:T(8,128)(2,1)} %convolution_convert_fusion), calls=%async_computation.3 | async-start | bytes 2097152 | tf_op jit(solution)/shard_map/all_to_all | solution.py:37
  57.0 0.0 reduce-scatter.3.cloned.1.call-start
  57.0 0.0 copy-start.2
  57.1 3.1 %fusion.10 = f32[8,16,512]{2,1,0:T(8,128)S(1)} fusion(bf16[8,16,4096]{2,1,0:T(8,128)(2,1)S(1)} %all-to-all-done, bf16[1,4096,512]{2,1,0:T(8,128)(2,1)} %param.12), kind=kOutput, calls=%fused_computation.15 | convolution fusion | flops 536870912 | bytes 5505024 | tf_op jit(solution)/shard_map/epf,fh->eph/dot_general | solution.py:72
  60.1 0.4 copy-done.2
  60.5 0.0 copy-start
  60.5 0.8 multiply_convert_fusion.2
  61.3 1.4 %copy-done = bf16[1,512,4096]{2,1,0:T(8,128)(2,1)S(1)} copy-done((bf16[1,512,4096]{2,1,0:T(8,128)(2,1)S(1)}, bf16[1,512,4096]{2,1,0:T(8,128)(2,1)}, u32[]{:S(2)}) %copy-start) | copy-done | bytes 4194328
  62.7 1.7 %convolution_convert_fusion.1 = bf16[8,16,4096]{2,1,0:T(8,128)(2,1)} fusion(bf16[8,16,512]{2,1,0:T(8,128)(2,1)S(1)} %get-tuple-element.6, bf16[1,512,4096]{2,1,0:T(8,128)(2,1)S(1)} %copy-done), kind=kOutput, calls=%fused_computation.5 | convolution fusion | flops 537395200 | bytes 5373952 | tf_op jit(solution)/shard_map/eph,hf->epf/dot_general | solution.py:80
  64.4 0.0 reduce-scatter.3.cloned.1.call-update
  64.4 0.0 reduce-scatter.5.cloned.1.call-start
  64.5 7.9 %all-to-all-done.2 = bf16[8,16,4096]{2,1,0:T(8,128)(2,1)S(1)} async-done(((bf16[8,16,4096]{2,1,0:T(8,128)(2,1)}), bf16[8,16,4096]{2,1,0:T(8,128)(2,1)S(1)}, u32[]{:S(2)}, u32[]{:S(2)}) %all-to-all-start.2) | async-done | bytes 1048608 | tf_op jit(solution)/shard_map/all_to_all | solution.py:37
  72.4 0.0 copy-start.1
  72.4 3.9 %fusion.2 = f32[8,16,512]{2,1,0:T(8,128)S(1)} fusion(bf16[8,16,4096]{2,1,0:T(8,128)(2,1)S(1)} %all-to-all-done.2, bf16[1,512,4096]{2,1,0:T(8,128)(2,1)} %param.14), kind=kOutput, calls=%fused_computation.7 | convolution fusion | flops 536870912 | bytes 5505024 | tf_op jit(solution)/shard_map/epf,hf->eph/dot_general | solution.py:87
  76.3 0.0 copy-start.3
  76.3 0.0 copy-done.1
  76.3 1.5 %fusion.8 = f32[8,16,4096]{2,1,0:T(8,128)S(1)} fusion(bf16[1,4096,512]{2,1,0:T(8,128)(2,1)S(1)} %copy-done.1, f32[8,16,512]{2,1,0:T(8,128)S(1)} %fusion.10, f32[8,16,512]{2,1,0:T(8,128)S(1)} %fusion.2, f32[8,16,512]{2,1,0:T(8,128)S(1)} %get-tuple-element.7), kind=kOutput, calls=%fused_computation.13 | convolution fusion | flops 537526272 | bytes 7077888 | tf_op jit(solution)/shard_map/eph,fh->epf/dot_general | solution.py:99
  77.8 0.7 copy-done.3
  78.5 2.5 %fusion.1 = bf16[8,16,4096]{2,1,0:T(8,128)(2,1)} fusion(f32[8,16,4096]{2,1,0:T(8,128)S(1)} %fusion.8, bf16[1,4096,512]{2,1,0:T(8,128)(2,1)S(1)} %copy-done.3, f32[8,16,512]{2,1,0:T(8,128)S(1)} %fusion.2, f32[8,16,512]{2,1,0:T(8,128)S(1)} %fusion.10), kind=kOutput, calls=%fused_computation.3 | convolution fusion | flops 538312704 | bytes 7864320 | tf_op jit(solution)/shard_map/eph,fh->epf/dot_general | solution.py:102
  81.0 0.0 reduce-scatter.5.cloned.1.call-update
  81.0 9.4 %reduce-scatter.3.cloned.1.call-done = bf16[8,16,1024]{2,1,0:T(8,128)(2,1)} async-done(((bf16[8,16,4096]{2,1,0:T(8,128)(2,1)}), bf16[8,16,1024]{2,1,0:T(8,128)(2,1)}) %reduce-scatter.3.cloned.1.call-update) | async-done | bytes 262160 | tf_op jit(solution)/shard_map/reduce_scatter | solution.py:42
  90.4 3.7 %all-to-all-start.1 = ((bf16[8,16,1024]{2,1,0:T(8,128)(2,1)}), bf16[8,16,1024]{2,1,0:T(8,128)(2,1)S(1)}, u32[]{:S(2)}, u32[]{:S(2)}) async-start(bf16[8,16,1024]{2,1,0:T(8,128)(2,1)} %reduce-scatter.3.cloned.1.call-done), calls=%async_computation.2 | async-start | bytes 524288 | tf_op jit(solution)/shard_map/all_to_all | solution.py:45
  94.1 3.3 %fusion = bf16[1,512,4096]{2,1,0:T(8,128)(2,1)} fusion(bf16[8,16,512]{2,1,0:T(8,128)(2,1)S(1)} %get-tuple-element.6, bf16[8,16,4096]{2,1,0:T(8,128)(2,1)S(1)} %all-to-all-done.2), kind=kOutput, calls=%fused_computation.1 | convolution fusion | flops 538968064 | bytes 5373952 | tf_op jit(solution)/shard_map/eph,epf->hf/dot_general | solution.py:88
  97.3 21.2 %reduce-scatter.5.cloned.1.call-done = bf16[8,16,1024]{2,1,0:T(8,128)(2,1)} async-done(((bf16[8,16,4096]{2,1,0:T(8,128)(2,1)}), bf16[8,16,1024]{2,1,0:T(8,128)(2,1)}) %reduce-scatter.5.cloned.1.call-update) | async-done | bytes 262160 | tf_op jit(solution)/shard_map/reduce_scatter | solution.py:42
  118.6 0.0 all-to-all-done.1
  118.6 3.7 %all-to-all-start.3 = ((bf16[8,16,1024]{2,1,0:T(8,128)(2,1)}), bf16[8,16,1024]{2,1,0:T(8,128)(2,1)S(1)}, u32[]{:S(2)}, u32[]{:S(2)}) async-start(bf16[8,16,1024]{2,1,0:T(8,128)(2,1)} %reduce-scatter.5.cloned.1.call-done), calls=%async_computation.5 | async-start | bytes 524288 | tf_op jit(solution)/shard_map/all_to_all | solution.py:45
  122.3 1.1 fusion.12
  123.4 5.8 %all-to-all-done.3 = bf16[8,16,1024]{2,1,0:T(8,128)(2,1)S(1)} async-done(((bf16[8,16,1024]{2,1,0:T(8,128)(2,1)}), bf16[8,16,1024]{2,1,0:T(8,128)(2,1)S(1)}, u32[]{:S(2)}, u32[]{:S(2)}) %all-to-all-start.3) | async-done | bytes 262176 | tf_op jit(solution)/shard_map/all_to_all | solution.py:45
  129.2 1.1 fusion.13
  (1 shorter events, 0.0 us)
Async XLA Ops:
  7.2 7.2 %collective-permute-start = (bf16[16,1024]{1,0:T(8,128)(2,1)}, bf16[16,1024]{1,0:T(8,128)(2,1)S(1)}, u32[]{:S(2)}, u32[]{:S(2)}) collective-permute-start(bf16[16,1024]{1,0:T(8,128)(2,1)} %param.9), channel_id=1, source_target_pairs={{0,1},{1,2},{2,3},{3,0},{4,5},{5,6},{6,7},{7,4},{8,9},{9,10},{10,1... | collective-permute-start | bytes 98312 | tf_op jit(solution)/shard_map/ppermute | solution.py:33
  14.4 5.7 %collective-permute-start.1 = (bf16[16,1024]{1,0:T(8,128)(2,1)S(1)}, bf16[16,1024]{1,0:T(8,128)(2,1)S(1)}, u32[]{:S(2)}, u32[]{:S(2)}) collective-permute-start(bf16[16,1024]{1,0:T(8,128)(2,1)S(1)} %collective-permute-done), channel_id=1, source_target_pairs={{0,1},{1,2},{2,3},{3,0},{4,5},{5,6},{6,7},{7,4},{8,9},{9,10},{10,1... | collective-permute-start | bytes 98312 | tf_op jit(solution)/shard_map/ppermute | solution.py:33
  20.1 5.7 %collective-permute-start.2 = (bf16[16,1024]{1,0:T(8,128)(2,1)S(1)}, bf16[16,1024]{1,0:T(8,128)(2,1)S(1)}, u32[]{:S(2)}, u32[]{:S(2)}) collective-permute-start(bf16[16,1024]{1,0:T(8,128)(2,1)S(1)} %collective-permute-done.1), channel_id=1, source_target_pairs={{0,1},{1,2},{2,3},{3,0},{4,5},{5,6},{6,7},{7,4},{8,9},{9,10},{10,1... | collective-permute-start | bytes 98312 | tf_op jit(solution)/shard_map/ppermute | solution.py:33
  28.4 24.4 %all-to-all-start = ((bf16[8,16,4096]{2,1,0:T(8,128)(2,1)}), bf16[8,16,4096]{2,1,0:T(8,128)(2,1)S(1)}, u32[]{:S(2)}, u32[]{:S(2)}) async-start(bf16[8,16,4096]{2,1,0:T(8,128)(2,1)} %convolution_convert_fusion.2), calls=%async_computation | async-start | bytes 2097152 | tf_op jit(solution)/shard_map/all_to_all | solution.py:37
  32.3 5.9 %collective-permute-start.3 = (bf16[16,1024]{1,0:T(8,128)(2,1)}, bf16[16,1024]{1,0:T(8,128)(2,1)S(1)}, u32[]{:S(2)}, u32[]{:S(2)}) collective-permute-start(bf16[16,1024]{1,0:T(8,128)(2,1)} %param.15), channel_id=1, source_target_pairs={{0,1},{1,2},{2,3},{3,0},{4,5},{5,6},{6,7},{7,4},{8,9},{9,10},{10,1... | collective-permute-start | bytes 98312 | tf_op jit(solution)/shard_map/ppermute | solution.py:33
  38.2 5.7 %collective-permute-start.4 = (bf16[16,1024]{1,0:T(8,128)(2,1)S(1)}, bf16[16,1024]{1,0:T(8,128)(2,1)S(1)}, u32[]{:S(2)}, u32[]{:S(2)}) collective-permute-start(bf16[16,1024]{1,0:T(8,128)(2,1)S(1)} %collective-permute-done.3), channel_id=1, source_target_pairs={{0,1},{1,2},{2,3},{3,0},{4,5},{5,6},{6,7},{7,4},{8,9},{9,10},{10,1... | collective-permute-start | bytes 98312 | tf_op jit(solution)/shard_map/ppermute | solution.py:33
  43.9 5.7 %collective-permute-start.5 = (bf16[16,1024]{1,0:T(8,128)(2,1)S(1)}, bf16[16,1024]{1,0:T(8,128)(2,1)S(1)}, u32[]{:S(2)}, u32[]{:S(2)}) collective-permute-start(bf16[16,1024]{1,0:T(8,128)(2,1)S(1)} %collective-permute-done.4), channel_id=1, source_target_pairs={{0,1},{1,2},{2,3},{3,0},{4,5},{5,6},{6,7},{7,4},{8,9},{9,10},{10,1... | collective-permute-start | bytes 98312 | tf_op jit(solution)/shard_map/ppermute | solution.py:33
  52.8 19.6 %all-to-all-start.2 = ((bf16[8,16,4096]{2,1,0:T(8,128)(2,1)}), bf16[8,16,4096]{2,1,0:T(8,128)(2,1)S(1)}, u32[]{:S(2)}, u32[]{:S(2)}) async-start(bf16[8,16,4096]{2,1,0:T(8,128)(2,1)} %convolution_convert_fusion), calls=%async_computation.3 | async-start | bytes 2097152 | tf_op jit(solution)/shard_map/all_to_all | solution.py:37
  57.0 33.4 %reduce-scatter.3.cloned.1.call-start = ((), (), s32[]{:S(2)}) async-start(), calls=%async_computation.6 | async-start | bytes 1310720 | tf_op jit(solution)/shard_map/reduce_scatter | solution.py:42
  57.0 3.5 %copy-start.2 = (bf16[1,4096,512]{2,1,0:T(8,128)(2,1)S(1)}, bf16[1,4096,512]{2,1,0:T(8,128)(2,1)}, u32[]{:S(2)}) copy-start(bf16[1,4096,512]{2,1,0:T(8,128)(2,1)} %param.13) | copy-start | bytes 12582916
  60.5 2.2 %copy-start = (bf16[1,512,4096]{2,1,0:T(8,128)(2,1)S(1)}, bf16[1,512,4096]{2,1,0:T(8,128)(2,1)}, u32[]{:S(2)}) copy-start(bf16[1,512,4096]{2,1,0:T(8,128)(2,1)} %param.14) | copy-start | bytes 12582916
  64.4 54.1 %reduce-scatter.5.cloned.1.call-start = ((), (), s32[]{:S(2)}) async-start(), calls=%async_computation.7 | async-start | bytes 1310720 | tf_op jit(solution)/shard_map/reduce_scatter | solution.py:42
  72.4 3.9 %copy-start.1 = (bf16[1,4096,512]{2,1,0:T(8,128)(2,1)S(1)}, bf16[1,4096,512]{2,1,0:T(8,128)(2,1)}, u32[]{:S(2)}) copy-start(bf16[1,4096,512]{2,1,0:T(8,128)(2,1)} %param.12) | copy-start | bytes 12582916
  76.3 2.2 %copy-start.3 = (bf16[1,4096,512]{2,1,0:T(8,128)(2,1)S(1)}, bf16[1,4096,512]{2,1,0:T(8,128)(2,1)}, u32[]{:S(2)}) copy-start(bf16[1,4096,512]{2,1,0:T(8,128)(2,1)} %param.13) | copy-start | bytes 12582916
  90.4 28.2 %all-to-all-start.1 = ((bf16[8,16,1024]{2,1,0:T(8,128)(2,1)}), bf16[8,16,1024]{2,1,0:T(8,128)(2,1)S(1)}, u32[]{:S(2)}, u32[]{:S(2)}) async-start(bf16[8,16,1024]{2,1,0:T(8,128)(2,1)} %reduce-scatter.3.cloned.1.call-done), calls=%async_computation.2 | async-start | bytes 524288 | tf_op jit(solution)/shard_map/all_to_all | solution.py:45
  118.6 10.6 %all-to-all-start.3 = ((bf16[8,16,1024]{2,1,0:T(8,128)(2,1)}), bf16[8,16,1024]{2,1,0:T(8,128)(2,1)S(1)}, u32[]{:S(2)}, u32[]{:S(2)}) async-start(bf16[8,16,1024]{2,1,0:T(8,128)(2,1)} %reduce-scatter.5.cloned.1.call-done), calls=%async_computation.5 | async-start | bytes 524288 | tf_op jit(solution)/shard_map/all_to_all | solution.py:45
Sparse Core Ops, SparseCore 0:
  64.6 25.7 reduce-scatter.2
  92.8 25.7 reduce-scatter.4
